TPU v7x, 512 devices: a whole 4x4x16 slice. The times are simulated.
512 devices in a mesh: bricks: 512 (over y, x, z, core).
Axes of the slice: x: 4, y: 4, z: 16, core: 2. Of those that a mesh axis runs over, the one named last changes fastest.
Arguments:
- density: bfloat16 [512, 4, 128, 256], P('bricks'), may hold values from -6 to 6
- material: int32 [512, 4, 128, 256], P('bricks'), may hold values from 0 to 7
- colour_table: float32 [8, 3], replicated, may hold values from 0.1 to 1
- opacity_table: float32 [8], replicated, may hold values from 0.002 to 0.04
- centre_table: float32 [8], replicated, may hold values from -1 to 1
- slice_weights: float32 [512, 4, 4], P('bricks'), may hold values from 0.1 to 1
- front_flags: int32 [512, 5], P('bricks'), may hold values from 0 to 1, as said below
Outputs:
- frame: float32 [4, 512, 2048], P(None, 'bricks')
Inputs may be any that keep to these rules, and one draw needn't show every extreme that they name: `front_flags`: the last column is the same for every brick. Column k < 4 equals bit k of bx XOR that last column, with bx = brick index // 32.
All inputs are finite; a program needn't handle non-finite values.
Results may differ from a plain program's by a relative error of at most 0.0012.
Values may be sent and summed in bfloat16 or wider, within the bound.
A program may use at most 64 MiB of HBM per device.

v0:
```python
import jax
import jax.numpy as jnp
from jax import lax
from jax.experimental import pallas as pl
from jax.experimental.pallas import tpu as pltpu
from jax.sharding import PartitionSpec as P

GX = 16
GY = 16
GZ = 2
MATS = 8
CX = 4
CY = 128
CZ = 256
SLAB = CY // 2
MESH = pl.DeviceIdType.MESH
SCALE = 2.0**20


def place(bx, by, bz):
    return ((bx * GY + by) * GZ + bz,)


def kernel(
    den, mat, col, opa, cen, wts, flg, out,
    dbuf, mbuf, wbuf, col_s, opa_s, cen_s, flg_s, wrep, tabs, qbuf, row_out, row_in, sbuf, rbuf,
    local_sems, core_send, core_recv, face_send, face_recv, edge_send, edge_recv,
    row_sems, part_send, part_recv,
):
    me = lax.axis_index("bricks")
    bx = me // (GY * GZ)
    by = (me // GZ) % GY
    c = me % GZ
    other = 1 - c

    own_rows = pl.multiple_of(c * 48, 16)
    own_dst = pl.multiple_of(other * 16, 16)
    own_mat = pl.multiple_of(c * SLAB, 16)
    locals_ = [
        pltpu.make_async_copy(
            den.at[0, :, pl.ds(own_rows, 80), :],
            dbuf.at[c, pl.ds(1, CX), pl.ds(own_dst, 80), :],
            local_sems.at[0],
        ),
        pltpu.make_async_copy(
            mat.at[0, :, pl.ds(own_mat, SLAB), :], mbuf.at[c], local_sems.at[1]
        ),
        pltpu.make_async_copy(wts.at[0], wbuf.at[c], local_sems.at[2]),
        pltpu.make_async_copy(col, col_s, local_sems.at[3]),
        pltpu.make_async_copy(opa, opa_s, local_sems.at[4]),
        pltpu.make_async_copy(cen, cen_s, local_sems.at[5]),
        pltpu.make_async_copy(flg, flg_s, local_sems.at[6]),
    ]
    for copy in locals_:
        copy.start()

    barrier = pltpu.get_barrier_semaphore()

    def tell(target):
        pl.semaphore_signal(barrier, inc=1, device_id=target, device_id_type=MESH)

    tell(place(bx, by, other))

    @pl.when(bx > 0)
    def _():
        tell(place(bx - 1, by, 0))
        tell(place(bx - 1, by, 1))

    @pl.when(bx < GX - 1)
    def _():
        tell(place(bx + 1, by, 0))
        tell(place(bx + 1, by, 1))

    @pl.when((c == 0) & (by > 0))
    def _():
        tell(place(bx, by - 1, 0))
        tell(place(bx, by - 1, 1))

    @pl.when((c == 1) & (by < GY - 1))
    def _():
        tell(place(bx, by + 1, 0))
        tell(place(bx, by + 1, 1))

    source_core = bx // 8
    keeps_own = source_core == c

    def tell_part(k, _):
        @pl.when(jnp.logical_not(keeps_own & (k == bx)))
        def _():
            tell(place(k, by, source_core))

        return 0

    lax.fori_loop(0, GX, tell_part, 0)

    @pl.when(bx == 0)
    def _():
        dbuf[:, 0] = jnp.zeros(dbuf.shape[:1] + dbuf.shape[2:], dbuf.dtype)

    @pl.when(bx == GX - 1)
    def _():
        dbuf[:, CX + 1] = jnp.zeros(dbuf.shape[:1] + dbuf.shape[2:], dbuf.dtype)

    @pl.when((c == 0) & (by == 0))
    def _():
        dbuf[:, 1 : CX + 1, 0:16, :] = jnp.zeros((GZ, CX, 16, CZ), dbuf.dtype)

    last_slab = (c == 1) & (by == GY - 1)

    @pl.when(last_slab)
    def _():
        dbuf[:, 1 : CX + 1, 80:96, :] = jnp.zeros((GZ, CX, 16, CZ), dbuf.dtype)
        row_in[...] = jnp.zeros(row_in.shape, row_in.dtype)

    peers = 16 + 2 * jnp.minimum(bx, 1) + 2 * jnp.minimum(GX - 1 - bx, 1)
    peers = peers + jnp.minimum(by, 1) + jnp.minimum(GY - 1 - by, 1)
    peers = peers + (source_core + c) % 2
    pl.semaphore_wait(barrier, peers)

    def remote(src, dst, send, recv, target):
        return pltpu.make_async_remote_copy(
            src_ref=src, dst_ref=dst, send_sem=send, recv_sem=recv,
            device_id=target, device_id_type=MESH,
        )

    up_faces = [
        remote(
            den.at[0, CX - 1, pl.ds(h * SLAB, SLAB), :],
            dbuf.at[c, 0, pl.ds(16, SLAB), :],
            face_send.at[h], face_recv.at[c], place(bx + 1, by, h),
        )
        for h in range(2)
    ]
    down_faces = [
        remote(
            den.at[0, 0, pl.ds(h * SLAB, SLAB), :],
            dbuf.at[c, CX + 1, pl.ds(16, SLAB), :],
            face_send.at[2 + h], face_recv.at[2 + c], place(bx - 1, by, h),
        )
        for h in range(2)
    ]

    @pl.when(bx < GX - 1)
    def _():
        for copy in up_faces:
            copy.start()

    @pl.when(bx > 0)
    def _():
        for copy in down_faces:
            copy.start()

    away_rows = pl.multiple_of(other * 48, 16)
    away_dst = pl.multiple_of(c * 16, 16)
    away_mat = pl.multiple_of(other * SLAB, 16)
    swaps = [
        remote(
            den.at[0, :, pl.ds(away_rows, 80), :],
            dbuf.at[c, pl.ds(1, CX), pl.ds(away_dst, 80), :],
            core_send.at[0], core_recv.at[0], place(bx, by, other),
        ),
        remote(
            mat.at[0, :, pl.ds(away_mat, SLAB), :], mbuf.at[c],
            core_send.at[1], core_recv.at[1], place(bx, by, other),
        ),
        remote(wts.at[0], wbuf.at[c], core_send.at[2], core_recv.at[2], place(bx, by, other)),
    ]
    for copy in swaps:
        copy.start()

    last_rows = remote(
        den.at[0, :, pl.ds(CY - 16, 16), :], dbuf.at[c, pl.ds(1, CX), pl.ds(0, 16), :],
        edge_send.at[0], edge_recv.at[c], place(bx, by + 1, 0),
    )
    first_rows = remote(
        den.at[0, :, pl.ds(0, 16), :], dbuf.at[c, pl.ds(1, CX), pl.ds(80, 16), :],
        edge_send.at[1], edge_recv.at[c], place(bx, by - 1, 1),
    )

    @pl.when(by < GY - 1)
    def _():
        last_rows.start()

    @pl.when(by > 0)
    def _():
        first_rows.start()

    for copy in locals_:
        copy.wait()

    rows8 = lax.broadcasted_iota(jnp.int32, (8, 128), 0)

    def spread(entry):
        full = jnp.zeros((8, 128), jnp.float32)
        for k in range(MATS):
            full = jnp.where(rows8 == k, entry(k), full)
        return full

    tabs[0] = spread(lambda k: opa_s[k])
    tabs[1] = spread(lambda k: cen_s[k])
    for ch in range(3):
        tabs[2 + ch] = spread(lambda k, ch=ch: col_s[ch, k])

    swaps[2].wait_recv()
    for b in range(GZ):
        weights = wbuf[b]
        weights = weights / jnp.sum(weights, axis=1, keepdims=True)
        for s in range(CX):
            for k in range(4):
                wrep[b, s * 4 + k] = jnp.broadcast_to(weights[s : s + 1, k : k + 1], (8, 128))

    swaps[0].wait_recv()
    swaps[1].wait_recv()

    @pl.when(((c == 0) & (by > 0)) | ((c == 1) & (by < GY - 1)))
    def _():
        for b in range(GZ):
            remote(
                den.at[0, :, pl.ds(0, 16), :], dbuf.at[b, pl.ds(1, CX), pl.ds(0, 16), :],
                edge_send.at[0], edge_recv.at[b], place(bx, by, other),
            ).wait_recv()

    def wait_face(which, b):
        remote(
            den.at[0, 0, pl.ds(0, SLAB), :], dbuf.at[b, 0, pl.ds(16, SLAB), :],
            face_send.at[0], face_recv.at[2 * which + b], place(bx, by, other),
        ).wait_recv()

    @pl.when(bx > 0)
    def _():
        for b in range(GZ):
            wait_face(0, b)

    @pl.when(bx < GX - 1)
    def _():
        for b in range(GZ):
            wait_face(1, b)

    lane512 = lax.broadcasted_iota(jnp.int32, (16, 2 * CZ), 1)
    row16 = lax.broadcasted_iota(jnp.int32, (16, 2 * CZ), 0)
    lane128 = lax.broadcasted_iota(jnp.int32, (8, 128), 1)

    def lookup(kinds):
        found = [[] for _ in range(5)]
        for r in range(2):
            parts = [[] for _ in range(5)]
            for lc in range(4):
                index = kinds[r * 8 : r * 8 + 8, lc * 128 : lc * 128 + 128]
                for t in range(5):
                    parts[t].append(jnp.take_along_axis(tabs[t], index, axis=0))
            for t in range(5):
                found[t].append(jnp.concatenate(parts[t], axis=1))
        return [jnp.concatenate(f, axis=0) for f in found]

    def shade(p):
        base = pl.multiple_of(16 * p, 16)

        def load(sl, start):
            halves = [dbuf[b, sl, pl.ds(start, 16), :] for b in range(GZ)]
            return jnp.concatenate(halves, axis=1).astype(jnp.float32)

        for s in range(CX):
            here = load(s + 1, base + 16)
            above = load(s + 1, base)
            below = load(s + 1, base + 32)
            gx = load(s + 2, base + 16) - load(s, base + 16)
            up = jnp.where(row16 == 15, pltpu.roll(below, 15, 0), pltpu.roll(here, 15, 0))
            down = jnp.where(row16 == 0, pltpu.roll(above, 1, 0), pltpu.roll(here, 1, 0))
            gy = up - down
            right = jnp.where(lane512 == 2 * CZ - 1, 0.0, pltpu.roll(here, 2 * CZ - 1, 1))
            left = jnp.where(lane512 == 0, 0.0, pltpu.roll(here, 1, 1))
            gz = right - left
            kinds = jnp.concatenate([mbuf[b, s, pl.ds(base, 16), :] for b in range(GZ)], axis=1)
            opacity, centre, red, green, blue = lookup(kinds)
            absorb = opacity / (1.0 + jnp.exp(2.0 * (centre - here)))
            squares = gx * gx + gy * gy + gz * gz
            facing = jnp.abs(0.3 * gx + 0.24 * gy + 0.32 * gz) * lax.rsqrt(0.25 * squares + 1.0)
            weight = (0.35 + 0.65 * facing) * absorb
            for ch, value in enumerate((red * weight, green * weight, blue * weight, absorb)):
                qbuf[s * 4 + ch, pl.ds(base, 16), :] = value

    shade(0)
    for k in range(16):
        row_out[k : k + 1, :] = qbuf[k, 0:1, :]

    row_target = jnp.where(c == 1, me - 1, me - 2 * 1 + 1)
    row_copy = remote(row_out, row_in, row_sems.at[0], row_sems.at[1], (row_target,))
    has_previous = (c == 1) | (by > 0)

    @pl.when(has_previous)
    def _():
        row_copy.start()

    def shade_step(p, _):
        shade(p)
        return 0

    lax.fori_loop(1, 4, shade_step, 0)

    @pl.when(jnp.logical_not(last_slab))
    def _():
        row_copy.wait_recv()

    for k in range(16):
        qbuf[k, SLAB : SLAB + 1, :] = row_in[k : k + 1, :]

    forward = flg_s[0, 4]
    j0 = bx % 8

    def group(i, _):
        j = (j0 + i) % 8
        base = pl.multiple_of(8 * j, 8)
        total = [[None] * 4 for _ in range(4)]
        passing = [None] * 4
        for order in range(CX):
            s = order * forward + (CX - 1 - order) * (1 - forward)
            for ch in (3, 0, 1, 2):
                now = [qbuf[s * 4 + ch, pl.ds(base, 8), pl.ds(lc * 128, 128)] for lc in range(4)]
                nxt = [
                    jnp.where(
                        rows8 == 7,
                        qbuf[s * 4 + ch, pl.ds(base + 8, 1), pl.ds(lc * 128, 128)],
                        pltpu.roll(now[lc], 7, 0),
                    )
                    for lc in range(4)
                ]
                w = [[wrep[b, s * 4 + k] for k in range(4)] for b in range(GZ)]
                near, far = [], []
                for lc in range(4):
                    b = lc // 2
                    near.append(w[b][0] * now[lc] + w[b][1] * nxt[lc])
                    far.append(pltpu.roll(w[b][2] * now[lc] + w[b][3] * nxt[lc], 127, 1))
                cross = pltpu.roll(w[0][2] * now[2] + w[0][3] * nxt[2], 127, 1)
                following = [far[1], cross, far[3], jnp.zeros((8, 128), jnp.float32)]
                for lc in range(4):
                    sample = near[lc] + jnp.where(lane128 == 127, following[lc], far[lc])
                    if ch == 3:
                        before = passing[lc]
                        passing[lc] = 1.0 - sample if before is None else before * (1.0 - sample)
                        held = before
                        if lc == 0:
                            befores = []
                        befores.append(held)
                    if befores[lc] is None:
                        total[ch][lc] = sample
                    else:
                        total[ch][lc] = total[ch][lc] + befores[lc] * sample
        for b in range(GZ):
            for pair in range(2):
                halves = []
                for ch in (2 * pair, 2 * pair + 1):
                    wide = jnp.concatenate([total[ch][2 * b], total[ch][2 * b + 1]], axis=1)
                    wide = wide * SCALE
                    wide = wide * wide
                    halves.append(wide * wide)
                sbuf[j, b, pl.ds(16 * pair, 16), :] = jnp.concatenate(halves, axis=0).astype(
                    jnp.bfloat16
                )
        target_x = 8 * c + j
        for b in range(GZ):
            mine = (target_x == bx) & (c == b)

            @pl.when(mine)
            def _(b=b):
                pltpu.make_async_copy(sbuf.at[j, b], rbuf.at[bx], local_sems.at[7]).start()

            @pl.when(jnp.logical_not(mine))
            def _(b=b):
                remote(
                    sbuf.at[j, b], rbuf.at[bx], part_send.at[j, b], part_recv.at[bx],
                    place(target_x, by, b),
                ).start()

        return 0

    lax.fori_loop(0, 8, group, 0)

    def take(k, _):
        own = keeps_own & (k == bx)

        @pl.when(own)
        def _():
            pltpu.make_async_copy(sbuf.at[0, 0], rbuf.at[k], local_sems.at[7]).wait()

        @pl.when(jnp.logical_not(own))
        def _():
            remote(
                sbuf.at[0, 0], rbuf.at[k], part_send.at[0, 0], part_recv.at[k], place(bx, by, other)
            ).wait_recv()

        return 0

    lax.fori_loop(0, GX, take, 0)

    def decode(values):
        return lax.rsqrt(lax.rsqrt(values.astype(jnp.float32)))

    def part(order):
        k = order * forward + (GX - 1 - order) * (1 - forward)
        return decode(rbuf[k]) * (1.0 / SCALE)

    first = part(0)
    acc = [first[8 * ch : 8 * ch + 8] for ch in range(4)]
    clear = 1.0 - acc[3]
    for order in range(1, GX):
        nxt = part(order)
        pieces = [nxt[8 * ch : 8 * ch + 8] for ch in range(4)]
        for ch in range(4):
            acc[ch] = acc[ch] + clear * pieces[ch]
        clear = clear * (1.0 - pieces[3])
    for ch in range(4):
        for lc in range(2):
            out[ch, pl.ds(lc, 8, 2), :] = acc[ch][:, lc * 128 : lc * 128 + 128]

    @pl.when(bx < GX - 1)
    def _():
        for copy in up_faces:
            copy.wait_send()

    @pl.when(bx > 0)
    def _():
        for copy in down_faces:
            copy.wait_send()

    for copy in swaps:
        copy.wait_send()

    @pl.when(by < GY - 1)
    def _():
        last_rows.wait_send()

    @pl.when(by > 0)
    def _():
        first_rows.wait_send()

    @pl.when(has_previous)
    def _():
        row_copy.wait_send()

    def sent(j, _):
        for b in range(GZ):

            @pl.when(jnp.logical_not((8 * c + j == bx) & (c == b)))
            def _(b=b):
                remote(
                    sbuf.at[j, b], rbuf.at[bx], part_send.at[j, b], part_recv.at[bx],
                    place(bx, by, other),
                ).wait_send()

        return 0

    lax.fori_loop(0, 8, sent, 0)


def body(density, material, colour_table, opacity_table, centre_table, slice_weights, front_flags):
    any_space = pl.BlockSpec(memory_space=pltpu.HBM)
    frame = pl.pallas_call(
        kernel,
        out_shape=jax.ShapeDtypeStruct((4, 16, 128), jnp.float32),
        in_specs=[any_space] * 7,
        out_specs=pl.BlockSpec(memory_space=pltpu.VMEM),
        scratch_shapes=[
            pltpu.VMEM((GZ, CX + 2, SLAB + 32, CZ), jnp.bfloat16),
            pltpu.VMEM((GZ, CX, SLAB, CZ), jnp.int32),
            pltpu.VMEM((GZ, CX, 4), jnp.float32),
            pltpu.SMEM((3, MATS), jnp.float32),
            pltpu.SMEM((MATS,), jnp.float32),
            pltpu.SMEM((MATS,), jnp.float32),
            pltpu.SMEM((1, 5), jnp.int32),
            pltpu.VMEM((GZ, 16, 8, 128), jnp.float32),
            pltpu.VMEM((5, 8, 128), jnp.float32),
            pltpu.VMEM((16, SLAB + 8, 2 * CZ), jnp.float32),
            pltpu.VMEM((16, 2 * CZ), jnp.float32),
            pltpu.VMEM((16, 2 * CZ), jnp.float32),
            pltpu.VMEM((8, GZ, 32, CZ), jnp.bfloat16),
            pltpu.VMEM((GX, 32, CZ), jnp.bfloat16),
            pltpu.SemaphoreType.DMA((8,)),
            pltpu.SemaphoreType.DMA((3,)),
            pltpu.SemaphoreType.DMA((3,)),
            pltpu.SemaphoreType.DMA((4,)),
            pltpu.SemaphoreType.DMA((4,)),
            pltpu.SemaphoreType.DMA((2,)),
            pltpu.SemaphoreType.DMA((2,)),
            pltpu.SemaphoreType.DMA((2,)),
            pltpu.SemaphoreType.DMA((8, GZ)),
            pltpu.SemaphoreType.DMA((GX,)),
        ],
        compiler_params=pltpu.CompilerParams(
            collective_id=0, has_side_effects=True, vmem_limit_bytes=64 * 2**20 - 2**16
        ),
    )(
        density, material, colour_table.T, opacity_table, centre_table, slice_weights, front_flags
    )
    return frame.reshape(4, 1, 2048)


def solution(mesh):
    in_specs = (
        P("bricks", None, None, None),
        P("bricks", None, None, None),
        P(),
        P(),
        P(),
        P("bricks", None, None),
        P("bricks", None),
    )
    out_specs = P(None, "bricks", None)
    return jax.shard_map(body, mesh=mesh, in_specs=in_specs, out_specs=out_specs, check_vma=False)
```

profile of v0, /device:TPU:1, one launch (start us, length us, event | category | flops | bytes accessed | tf_op | source)
XLA Modules:
  0.0 24.5 jit_solution(13495011248719384232)
XLA Ops:
  0.0 23.1 %shard_map.73 = f32[4,16,128]{2,1,0:T(8,128)} custom-call(bf16[1,4,128,256]{3,2,1,0:T(8,128)(2,1)} %den.1, s32[1,4,128,256]{3,2,1,0:T(8,128)} %mat.1, f32[3,8]{1,0:T(4,128)} %bitcast.3, f32[8]{0:T(128)} %opa.1, f32[8]{0:T(128)} %cen.1, f32[1,4,4]{2,1,0:T(4,128)} %wts.1, s32[1,5]{1,0:T(1,128)} %flg.1), custom_call_target="tpu_custom_call" | custom-call | tf_op jit(solution)/shard_map/pallas_call | solution.py:457
  23.1 1.4 %copy.10 = f32[4,1,2048]{2,1,0:T(1,128)} copy(f32[4,1,2048]{2,1,0:T(1,128)} %bitcast.2) | data formatting | bytes 65536
where the time goes:
time: 24.7 us; the launch traced here: 24.5 us
  Pallas kernels  23.1 us (94%)
  local copies, waits for them, and re-layouts  1.38 us (6%)
    pallas_call x1, Pallas kernels, body(): pl.pallas_call(kernel, out_shape=jax.ShapeDtypeStruct((4, 16, 128), jnp.f...  23.1 us
    unnamed x1, local copies, waits for them, and re-layouts  1.38 us

commit v1 on v0

v1 whole, which is shorter than its diff:
```python
import jax
import jax.numpy as jnp
from jax import lax
from jax.experimental import pallas as pl
from jax.experimental.pallas import tpu as pltpu
from jax.sharding import PartitionSpec as P

GX = 16
GY = 16
GZ = 2
MATS = 8
CX = 4
CY = 128
CZ = 256
SLAB = CY // 2
MESH = pl.DeviceIdType.MESH
SCALE = 2.0**20
LOG2E = 1.4426950408889634


def place(bx, by, bz):
    return ((bx * GY + by) * GZ + bz,)


def kernel(
    den, mat, col, opa, cen, wts, flg, out,
    dbuf, mbuf, wbuf, col_s, opa_s, cen_s, flg_s, wrep, tabs, qbuf, held, mids, sbuf, rbuf,
    local_sems, core_send, core_recv, face_send, face_recv, edge_send, edge_recv,
    kind_recv, corner_recv, part_send, part_recv, relay, late,
):
    me = lax.axis_index("bricks")
    bx = me // (GY * GZ)
    by = (me // GZ) % GY
    c = me % GZ
    other = 1 - c

    barrier = pltpu.get_barrier_semaphore()

    def tell(target):
        pl.semaphore_signal(barrier, inc=1, device_id=target, device_id_type=MESH)

    source_core = bx // 8
    keeps_own = source_core == c
    column = bx % 4
    level = bx // 4
    ring = [
        level * 4 + (column + 1) % 4,
        level * 4 + (column + 3) % 4,
        ((level + 1) % 4) * 4 + column,
        ((level + 3) % 4) * 4 + column,
    ]
    @pl.when((c == 0) & (by > 0))
    def _():
        tell(place(bx, by - 1, 0))
        tell(place(bx, by - 1, 1))

    @pl.when((c == 1) & (by < GY - 1))
    def _():
        tell(place(bx, by + 1, 0))
        tell(place(bx, by + 1, 1))

        @pl.when(bx > 0)
        def _():
            tell(place(bx - 1, by + 1, 0))
            tell(place(bx - 1, by + 1, 1))

        @pl.when(bx < GX - 1)
        def _():
            tell(place(bx + 1, by + 1, 0))
            tell(place(bx + 1, by + 1, 1))

    latest = me == 0
    near_latest = (by == 0) & ((me == 1) | (bx == 1))

    @pl.when(jnp.logical_not(latest))
    def _():
        tell(place(bx, by, other))
        for near in ring:
            tell(place(near, by, 0))
            tell(place(near, by, 1))

    beside = (bx == 1) | (bx == 3) | (bx == 4) | (bx == 12)

    @pl.when((by == 0) & (bx > 0) & jnp.logical_not(beside))
    def _():
        tell(place(0, 0, 0))

    diagonals = [
        ((level + dy) % 4) * 4 + (column + dx) % 4 for dx in (1, 3) for dy in (1, 3)
    ]
    wraps_up = (column == 3) & (bx < GX - 1)
    wraps_down = (column == 0) & (bx > 0)

    @pl.when(wraps_up)
    def _():
        tell(place(bx + 1, by, 0))
        tell(place(bx + 1, by, 1))

    @pl.when(wraps_down)
    def _():
        tell(place(bx - 1, by, 0))
        tell(place(bx - 1, by, 1))

    own_rows = pl.multiple_of(c * 48, 16)
    own_dst = pl.multiple_of(other * 16, 16)
    own_mat = pl.multiple_of(c * 56, 8)
    own_mat_dst = pl.multiple_of(other * 8, 8)
    locals_ = [
        pltpu.make_async_copy(
            den.at[0, :, pl.ds(own_rows, 80), :],
            dbuf.at[c, pl.ds(1, CX), pl.ds(own_dst, 80), :],
            local_sems.at[0],
        ),
        pltpu.make_async_copy(
            mat.at[0, :, pl.ds(own_mat, 72), :],
            mbuf.at[c, :, pl.ds(own_mat_dst, 72), :],
            local_sems.at[1],
        ),
        pltpu.make_async_copy(wts.at[0], wbuf.at[c], local_sems.at[2]),
        pltpu.make_async_copy(col, col_s, local_sems.at[3]),
        pltpu.make_async_copy(opa, opa_s, local_sems.at[4]),
        pltpu.make_async_copy(cen, cen_s, local_sems.at[5]),
        pltpu.make_async_copy(flg, flg_s, local_sems.at[6]),
    ]
    for copy in locals_:
        copy.start()

    @pl.when(bx == 0)
    def _():
        dbuf[:, 0] = jnp.zeros(dbuf.shape[:1] + dbuf.shape[2:], dbuf.dtype)

    @pl.when(bx == GX - 1)
    def _():
        dbuf[:, CX + 1] = jnp.zeros(dbuf.shape[:1] + dbuf.shape[2:], dbuf.dtype)

    @pl.when((c == 0) & (by == 0))
    def _():
        dbuf[:, 1 : CX + 1, 0:16, :] = jnp.zeros((GZ, CX, 16, CZ), dbuf.dtype)

    last_slab = (c == 1) & (by == GY - 1)

    @pl.when(last_slab)
    def _():
        dbuf[:, 1 : CX + 1, 80:96, :] = jnp.zeros((GZ, CX, 16, CZ), dbuf.dtype)
        qbuf[:, SLAB:, :] = jnp.zeros((16, 8, 2 * CZ), jnp.float32)

    peers = 9 + jnp.minimum(by, 1) + jnp.minimum(GY - 1 - by, 1)
    peers = peers + 2 * (column // 3) * jnp.minimum(GX - 1 - bx, 1)
    peers = peers + 2 * ((3 - column) // 3) * jnp.minimum(bx, 1)
    peers = peers + jnp.minimum(by, 1) * (jnp.minimum(bx, 1) + jnp.minimum(GX - 1 - bx, 1))
    first = 1 - jnp.minimum(by, 1)
    ringed = 1 - jnp.minimum((bx - 1) * (bx - 1) * (bx - 3) * (bx - 3), 1)
    ringed = ringed + 1 - jnp.minimum((bx - 4) * (bx - 4) * (bx - 12) * (bx - 12), 1)
    sibling = c * (1 - jnp.minimum(bx, 1))
    peers = peers - first * (ringed + sibling)
    peers = peers + 22 * (1 - jnp.minimum(me, 1))
    pl.semaphore_wait(barrier, peers)

    def announce(target):
        pl.semaphore_signal(late, inc=1, device_id=target, device_id_type=MESH)

    @pl.when(latest)
    def _():
        announce(place(0, 0, 1))
        announce(place(1, 0, 0))
        announce(place(1, 0, 1))

    def remote(src, dst, send, recv, target):
        return pltpu.make_async_remote_copy(
            src_ref=src, dst_ref=dst, send_sem=send, recv_sem=recv,
            device_id=target, device_id_type=MESH,
        )

    away_rows = pl.multiple_of(other * 48, 16)
    away_dst = pl.multiple_of(c * 16, 16)
    away_mat = pl.multiple_of(other * 56, 8)
    away_mat_dst = pl.multiple_of(c * 8, 8)
    swaps = [
        remote(
            den.at[0, :, pl.ds(away_rows, 80), :],
            dbuf.at[c, pl.ds(1, CX), pl.ds(away_dst, 80), :],
            core_send.at[0], core_recv.at[0], place(bx, by, other),
        ),
        remote(
            mat.at[0, :, pl.ds(away_mat, 72), :], mbuf.at[c, :, pl.ds(away_mat_dst, 72), :],
            core_send.at[1], core_recv.at[1], place(bx, by, other),
        ),
        remote(wts.at[0], wbuf.at[c], core_send.at[2], core_recv.at[2], place(bx, by, other)),
    ]
    @pl.when(me != 1)
    def _():
        for copy in swaps:
            copy.start()

    up_faces = [
        remote(
            den.at[0, CX - 1, pl.ds(h * SLAB, 80 - 16 * h), :],
            dbuf.at[c, 0, pl.ds(16, 80 - 16 * h), :],
            face_send.at[h], face_recv.at[c], place(bx + 1, by, h),
        )
        for h in range(2)
    ]
    down_faces = [
        remote(
            den.at[0, 0, pl.ds(h * SLAB, 80 - 16 * h), :],
            dbuf.at[c, CX + 1, pl.ds(16, 80 - 16 * h), :],
            face_send.at[2 + h], face_recv.at[2 + c], place(bx - 1, by, h),
        )
        for h in range(2)
    ]

    @pl.when(bx < GX - 1)
    def _():
        for copy in up_faces:
            copy.start()

    @pl.when(bx > 0)
    def _():
        down_faces[1].start()

        @pl.when(jnp.logical_not(near_latest))
        def _():
            down_faces[0].start()

    last_rows = remote(
        den.at[0, :, pl.ds(CY - 16, 16), :], dbuf.at[c, pl.ds(1, CX), pl.ds(0, 16), :],
        edge_send.at[0], edge_recv.at[c], place(bx, by + 1, 0),
    )
    first_rows = remote(
        den.at[0, :, pl.ds(0, 16), :], dbuf.at[c, pl.ds(1, CX), pl.ds(80, 16), :],
        edge_send.at[1], edge_recv.at[c], place(bx, by - 1, 1),
    )

    first_kinds = remote(
        mat.at[0, :, pl.ds(0, 8), :], mbuf.at[c, :, pl.ds(72, 8), :],
        edge_send.at[2], kind_recv.at[c], place(bx, by - 1, 1),
    )
    up_corner = remote(
        den.at[0, CX - 1, pl.ds(0, 16), :], dbuf.at[c, 0, pl.ds(80, 16), :],
        edge_send.at[3], corner_recv.at[c], place(bx + 1, by - 1, 1),
    )
    down_corner = remote(
        den.at[0, 0, pl.ds(0, 16), :], dbuf.at[c, CX + 1, pl.ds(80, 16), :],
        edge_send.at[4], corner_recv.at[2 + c], place(bx - 1, by - 1, 1),
    )

    @pl.when(by < GY - 1)
    def _():
        last_rows.start()

    @pl.when(by > 0)
    def _():
        first_rows.start()

        @pl.when(bx < GX - 1)
        def _():
            up_corner.start()

        @pl.when(bx > 0)
        def _():
            down_corner.start()

        first_kinds.start()

    def pass_on(step, chips):
        @pl.when(jnp.logical_not(latest))
        def _():
            for near in chips:

                @pl.when((near * GY + by + c) != 0)
                def _(near=near):
                    pl.semaphore_signal(
                        relay.at[step], inc=1, device_id=place(near, by, c), device_id_type=MESH
                    )

        @pl.when(me == 1)
        def _():
            for near in chips:
                pl.semaphore_signal(
                    relay.at[step], inc=1, device_id=place(near, by, 0), device_id_type=MESH
                )

    def hear(step):
        @pl.when(jnp.logical_not(latest))
        def _():
            pl.semaphore_wait(relay.at[step], 4)

    @pl.when(latest)
    def _():
        for k in range(2, GX):
            announce(place(k, 0, 0))

    pass_on(0, ring)
    for copy in locals_:
        copy.wait()

    rows8 = lax.broadcasted_iota(jnp.int32, (8, 128), 0)

    def spread(entry):
        full = jnp.zeros((8, 128), jnp.float32)
        for k in range(MATS):
            full = jnp.where(rows8 == k, entry(k), full)
        return full

    tabs[0] = spread(lambda k: opa_s[k])
    tabs[1] = spread(lambda k: cen_s[k]) * (2.0 * LOG2E)
    for ch in range(3):
        tabs[2 + ch] = spread(lambda k, ch=ch: col_s[ch, k])

    hear(0)
    pass_on(1, diagonals)

    @pl.when(near_latest)
    def _():
        pl.semaphore_wait(late, 1)

        @pl.when(me == 1)
        def _():
            for copy in swaps:
                copy.start()

        @pl.when(me != 1)
        def _():
            down_faces[0].start()

    swaps[2].wait_recv()
    for b in range(GZ):
        weights = wbuf[b]
        weights = weights / jnp.sum(weights, axis=1, keepdims=True)
        for s in range(CX):
            for k in range(4):
                wrep[b, s * 4 + k] = jnp.broadcast_to(weights[s : s + 1, k : k + 1], (8, 128))

    swaps[0].wait_recv()
    swaps[1].wait_recv()

    rows512 = lax.broadcasted_iota(jnp.int32, (8, 2 * CZ), 0)
    lane128 = lax.broadcasted_iota(jnp.int32, (8, 128), 1)

    def shade(p, rows=16):
        base = pl.multiple_of(16 * p, 16)
        mat_base = pl.multiple_of(16 * p + 8, 8)

        def load(sl, start):
            halves = [dbuf[b, sl, pl.ds(start, 16), :] for b in range(GZ)]
            return jnp.concatenate(halves, axis=1).astype(jnp.float32)

        for s in range(CX):
            block = load(s + 1, base + 16)
            parts = [load(s + 1, base)[8:], block[:8], block[8:]]
            if rows == 16:
                parts.append(load(s + 1, base + 32)[:8])
            for r in range(rows // 8):
                at = pl.multiple_of(base + 8 * r, 8)
                here = parts[r + 1]
                up = jnp.where(
                    rows512 == 7, pltpu.roll(parts[r + 2], 7, 0), pltpu.roll(here, 7, 0)
                )
                down = jnp.where(
                    rows512 == 0, pltpu.roll(parts[r], 1, 0), pltpu.roll(here, 1, 0)
                )
                gy = up - down
                right = pltpu.roll(here, 2 * CZ - 1, 1)
                left = pltpu.roll(here, 1, 1)
                gz = jnp.concatenate(
                    [
                        right[:, :128] - jnp.where(lane128 == 0, 0.0, left[:, :128]),
                        right[:, 128:384] - left[:, 128:384],
                        jnp.where(lane128 == 127, 0.0, right[:, 384:]) - left[:, 384:],
                    ],
                    axis=1,
                )
                along = 0.24 * gy + 0.32 * gz
                squares = 0.25 * (gy * gy + gz * gz) + 1.0
                kinds = jnp.concatenate(
                    [
                        mbuf[b, s, pl.ds(pl.multiple_of(mat_base + 8 * r, 8), 8), :]
                        for b in range(GZ)
                    ],
                    axis=1,
                )

                def look(t):
                    return jnp.concatenate(
                        [
                            jnp.take_along_axis(
                                tabs[t], kinds[:, lc * 128 : lc * 128 + 128], axis=0
                            )
                            for lc in range(4)
                        ],
                        axis=1,
                    )

                below_one = 1.0 + jnp.exp2(look(1) - (2.0 * LOG2E) * here)
                inverse = pl.reciprocal(below_one, approx=True)
                absorb = look(0) * (inverse * (2.0 - below_one * inverse))
                weight = absorb
                if s in (1, 2):
                    gx = [
                        dbuf[b, s + 2, pl.ds(base + 16, 16), :].astype(jnp.float32)[8 * r : 8 * r + 8]
                        - dbuf[b, s, pl.ds(base + 16, 16), :].astype(jnp.float32)[8 * r : 8 * r + 8]
                        for b in range(GZ)
                    ]
                    gx = jnp.concatenate(gx, axis=1)
                    facing = jnp.abs(0.3 * gx + along) * lax.rsqrt(0.25 * (gx * gx) + squares)
                    weight = (0.35 + 0.65 * facing) * absorb
                else:
                    held[s // 3, 0, pl.ds(at, 8), :] = along
                    held[s // 3, 1, pl.ds(at, 8), :] = squares
                for ch in range(3):
                    qbuf[s * 4 + ch, pl.ds(at, 8), :] = look(2 + ch) * weight
                qbuf[s * 4 + 3, pl.ds(at, 8), :] = absorb

    def face_shade(p, rows=16):
        base = pl.multiple_of(16 * p, 16)

        def load(sl):
            halves = [dbuf[b, sl, pl.ds(base + 16, 16), :] for b in range(GZ)]
            return jnp.concatenate(halves, axis=1).astype(jnp.float32)[:rows]

        for s in (0, 3):
            gx = load(s + 2) - load(s)
            along = held[s // 3, 0, pl.ds(base, rows), :]
            squares = held[s // 3, 1, pl.ds(base, rows), :]
            facing = jnp.abs(0.3 * gx + along) * lax.rsqrt(0.25 * (gx * gx) + squares)
            factor = 0.35 + 0.65 * facing
            for ch in range(3):
                qbuf[s * 4 + ch, pl.ds(base, rows), :] = (
                    qbuf[s * 4 + ch, pl.ds(base, rows), :] * factor
                )

    forward = flg_s[0, 4]

    def slice_at(order):
        return order * forward + (CX - 1 - order) * (1 - forward)

    def resample(s, ch, base):
        now = [qbuf[s * 4 + ch, pl.ds(base, 8), pl.ds(lc * 128, 128)] for lc in range(4)]
        nxt = [
            jnp.where(
                rows8 == 7,
                qbuf[s * 4 + ch, pl.ds(base + 8, 1), pl.ds(lc * 128, 128)],
                pltpu.roll(now[lc], 7, 0),
            )
            for lc in range(4)
        ]
        w = [[wrep[b, s * 4 + k] for k in range(4)] for b in range(GZ)]
        near, far = [], []
        for lc in range(4):
            b = lc // 2
            near.append(w[b][0] * now[lc] + w[b][1] * nxt[lc])
            far.append(pltpu.roll(w[b][2] * now[lc] + w[b][3] * nxt[lc], 127, 1))
        cross = pltpu.roll(w[0][2] * now[2] + w[0][3] * nxt[2], 127, 1)
        following = [far[1], cross, far[3], jnp.zeros((8, 128), jnp.float32)]
        return [near[lc] + jnp.where(lane128 == 127, following[lc], far[lc]) for lc in range(4)]

    def middle(j):
        base = pl.multiple_of(8 * j, 8)
        opaque = [resample(slice_at(order), 3, base) for order in range(CX)]
        clear = [None, [], [], []]
        for lc in range(4):
            clear[1].append(1.0 - opaque[0][lc])
            clear[2].append(clear[1][lc] * (1.0 - opaque[1][lc]))
            clear[3].append(clear[2][lc] * (1.0 - opaque[2][lc]))
        for lc in range(4):
            lanes = pl.ds(lc * 128, 128)
            total = opaque[0][lc]
            for order in range(1, CX):
                total = total + clear[order][lc] * opaque[order][lc]
            mids[3, pl.ds(base, 8), lanes] = total
            mids[4, pl.ds(base, 8), lanes] = clear[3][lc]
        for ch in range(3):
            first = resample(slice_at(1), ch, base)
            second = resample(slice_at(2), ch, base)
            for lc in range(4):
                mids[ch, pl.ds(base, 8), pl.ds(lc * 128, 128)] = (
                    clear[1][lc] * first[lc] + clear[2][lc] * second[lc]
                )

    def middle_step(j, _):
        middle(j)
        return 0

    def shade_step(p, _):
        shade(p)
        return 0

    lax.fori_loop(1 - c, 4 - c, shade_step, 0)

    @pl.when(c == 0)
    def _():
        shade(4, 8)

    lax.fori_loop(2 - 2 * c, 8 - 3 * c, middle_step, 0)
    @pl.when(((c == 0) & (by > 0)) | ((c == 1) & (by < GY - 1)))
    def _():
        for b in range(GZ):
            remote(
                den.at[0, :, pl.ds(0, 16), :], dbuf.at[b, pl.ds(1, CX), pl.ds(0, 16), :],
                edge_send.at[0], edge_recv.at[b], place(bx, by, other),
            ).wait_recv()

    @pl.when((c == 1) & (by < GY - 1))
    def _():
        for b in range(GZ):
            remote(
                mat.at[0, :, pl.ds(0, 8), :], mbuf.at[b, :, pl.ds(72, 8), :],
                edge_send.at[2], kind_recv.at[b], place(bx, by, other),
            ).wait_recv()

    shade(3 * c)

    @pl.when((c == 1) & jnp.logical_not(last_slab))
    def _():
        shade(4, 8)

    lax.fori_loop(5 * c, 2 + 6 * c, middle_step, 0)

    def wait_face(which, b, rows):
        remote(
            den.at[0, 0, pl.ds(0, rows), :],
            dbuf.at[b, (CX + 1) * which, pl.ds(16, rows), :],
            face_send.at[0], face_recv.at[2 * which + b], place(bx, by, other),
        ).wait_recv()

    def wait_faces(which):
        for b in range(GZ):

            @pl.when(c == 1)
            def _(b=b):
                wait_face(which, b, SLAB)

            @pl.when(c == 0)
            def _(b=b):
                wait_face(which, b, 80)

    def wait_corners(which):
        for b in range(GZ):
            remote(
                den.at[0, 0, pl.ds(0, 16), :],
                dbuf.at[b, (CX + 1) * which, pl.ds(80, 16), :],
                face_send.at[0], corner_recv.at[2 * which + b], place(bx, by, other),
            ).wait_recv()

    @pl.when(bx > 0)
    def _():
        wait_faces(0)

    @pl.when(bx < GX - 1)
    def _():
        wait_faces(1)

    def face_step(p, _):
        face_shade(p)
        return 0

    same_half = 1 - (level // 2 + c) % 2
    far_level = (level + same_half) % 2

    def group(i, _):
        k = i % 4
        across = (2 - k) * (1 - k // 2) + (9 - 3 * k) * (k // 2)
        j = 4 * ((far_level + i // 4) % 2) + (column + across) % 4

        half = (far_level + i // 4) % 2
        later = i // 4

        @pl.when(k == 0)
        def _():
            lax.fori_loop(
                2 * half + later * half, 3 + half - later * (1 - half), face_step, 0
            )

        @pl.when((j == 7) & (c == 1) & (by < GY - 1))
        def _():
            @pl.when(bx > 0)
            def _():
                wait_corners(0)

            @pl.when(bx < GX - 1)
            def _():
                wait_corners(1)

        @pl.when((j == 7) & jnp.logical_not(last_slab))
        def _():
            face_shade(4, 8)

        base = pl.multiple_of(8 * j, 8)
        total = []
        for ch in range(3):
            first = resample(slice_at(0), ch, base)
            last = resample(slice_at(3), ch, base)
            total.append([
                first[lc]
                + mids[ch, pl.ds(base, 8), pl.ds(lc * 128, 128)]
                + mids[4, pl.ds(base, 8), pl.ds(lc * 128, 128)] * last[lc]
                for lc in range(4)
            ])
        total.append([mids[3, pl.ds(base, 8), pl.ds(lc * 128, 128)] for lc in range(4)])
        for b in range(GZ):
            for pair in range(2):
                halves = []
                for ch in (2 * pair, 2 * pair + 1):
                    wide = jnp.concatenate([total[ch][2 * b], total[ch][2 * b + 1]], axis=1)
                    wide = wide * SCALE
                    wide = wide * wide
                    halves.append(wide * wide)
                sbuf[2 * j + b, pl.ds(16 * pair, 16), :] = jnp.concatenate(halves, axis=0).astype(
                    jnp.bfloat16
                )

        @pl.when(i == 0)
        def _():
            hear(1)

        target_x = 8 * c + j

        for b in range(GZ):
            mine = (target_x == bx) & (c == b)

            @pl.when(mine)
            def _(b=b):
                pltpu.make_async_copy(sbuf.at[2 * j + b], rbuf.at[bx], part_recv).start()

            @pl.when(jnp.logical_not(mine) & (target_x + by + c + b > 0))
            def _(b=b):
                remote(
                    sbuf.at[2 * j + b], rbuf.at[bx], part_send, part_recv,
                    place(target_x, by, b),
                ).start()

        return 0

    lax.fori_loop(0, 8, group, 0)

    @pl.when((by + c == 0) & (bx > 0))
    def _():
        @pl.when(bx > 1)
        def _():
            pl.semaphore_wait(late, 1)

        remote(sbuf.at[0], rbuf.at[bx], part_send, part_recv, place(0, 0, 0)).start()

    remote(sbuf, rbuf, part_send, part_recv, place(bx, by, other)).wait_recv()

    def decode(values):
        return lax.rsqrt(lax.rsqrt(values.astype(jnp.float32)))

    def part(order):
        k = order * forward + (GX - 1 - order) * (1 - forward)
        return decode(rbuf[k]) * (1.0 / SCALE)

    first = part(0)
    acc = [first[8 * ch : 8 * ch + 8] for ch in range(4)]
    clear = 1.0 - acc[3]
    for order in range(1, GX):
        nxt = part(order)
        pieces = [nxt[8 * ch : 8 * ch + 8] for ch in range(4)]
        for ch in range(4):
            acc[ch] = acc[ch] + clear * pieces[ch]
        clear = clear * (1.0 - pieces[3])
    for ch in range(4):
        for lc in range(2):
            out[ch, pl.ds(lc, 8, 2), :] = acc[ch][:, lc * 128 : lc * 128 + 128]

    @pl.when(bx < GX - 1)
    def _():
        for copy in up_faces:
            copy.wait_send()

    @pl.when(bx > 0)
    def _():
        for copy in down_faces:
            copy.wait_send()

    for copy in swaps:
        copy.wait_send()

    @pl.when(by < GY - 1)
    def _():
        last_rows.wait_send()

    @pl.when(by > 0)
    def _():
        first_rows.wait_send()
        first_kinds.wait_send()

        @pl.when(bx < GX - 1)
        def _():
            up_corner.wait_send()

        @pl.when(bx > 0)
        def _():
            down_corner.wait_send()

    @pl.when(keeps_own)
    def _():
        remote(
            sbuf.at[pl.ds(0, 15)], rbuf.at[pl.ds(0, 15)], part_send, part_recv,
            place(bx, by, other),
        ).wait_send()

    @pl.when(jnp.logical_not(keeps_own))
    def _():
        remote(sbuf, rbuf, part_send, part_recv, place(bx, by, other)).wait_send()


def body(density, material, colour_table, opacity_table, centre_table, slice_weights, front_flags):
    any_space = pl.BlockSpec(memory_space=pltpu.HBM)
    frame = pl.pallas_call(
        kernel,
        out_shape=jax.ShapeDtypeStruct((4, 16, 128), jnp.float32),
        in_specs=[any_space] * 7,
        out_specs=pl.BlockSpec(memory_space=pltpu.VMEM),
        scratch_shapes=[
            pltpu.VMEM((GZ, CX + 2, SLAB + 32, CZ), jnp.bfloat16),
            pltpu.VMEM((GZ, CX, SLAB + 16, CZ), jnp.int32),
            pltpu.VMEM((GZ, CX, 4), jnp.float32),
            pltpu.SMEM((3, MATS), jnp.float32),
            pltpu.SMEM((MATS,), jnp.float32),
            pltpu.SMEM((MATS,), jnp.float32),
            pltpu.SMEM((1, 5), jnp.int32),
            pltpu.VMEM((GZ, 16, 8, 128), jnp.float32),
            pltpu.VMEM((5, 8, 128), jnp.float32),
            pltpu.VMEM((16, SLAB + 8, 2 * CZ), jnp.float32),
            pltpu.VMEM((2, 2, SLAB + 8, 2 * CZ), jnp.float32),
            pltpu.VMEM((5, SLAB, 2 * CZ), jnp.float32),
            pltpu.VMEM((16, 32, CZ), jnp.bfloat16),
            pltpu.VMEM((GX, 32, CZ), jnp.bfloat16),
            pltpu.SemaphoreType.DMA((8,)),
            pltpu.SemaphoreType.DMA((3,)),
            pltpu.SemaphoreType.DMA((3,)),
            pltpu.SemaphoreType.DMA((4,)),
            pltpu.SemaphoreType.DMA((4,)),
            pltpu.SemaphoreType.DMA((5,)),
            pltpu.SemaphoreType.DMA((2,)),
            pltpu.SemaphoreType.DMA((2,)),
            pltpu.SemaphoreType.DMA((4,)),
            pltpu.SemaphoreType.DMA,
            pltpu.SemaphoreType.DMA,
            pltpu.SemaphoreType.REGULAR((2,)),
            pltpu.SemaphoreType.REGULAR,
        ],
        compiler_params=pltpu.CompilerParams(
            collective_id=0, has_side_effects=True, vmem_limit_bytes=32 * 2**20
        ),
    )(*[
        pltpu.with_memory_space_constraint(x, pltpu.HBM)
        for x in (
            density, material, colour_table.T, opacity_table, centre_table, slice_weights,
            front_flags,
        )
    ])
    return frame.reshape(4, 1, 2048)


def solution(mesh):
    in_specs = (
        P("bricks", None, None, None),
        P("bricks", None, None, None),
        P(),
        P(),
        P(),
        P("bricks", None, None),
        P("bricks", None),
    )
    out_specs = P(None, "bricks", None)
    return jax.shard_map(body, mesh=mesh, in_specs=in_specs, out_specs=out_specs, check_vma=False)
```

time: 24.7 us -> 19.1 us (0.77)
  the two profiles are of different devices: /device:TPU:1 before, /device:TPU:225 now
where the time goes in v1:
time: 19.1 us; the launch traced here: 18.9 us
  Pallas kernels  18.3 us (96%)
  local copies, waits for them, and re-layouts  0.62 us (3%)
    pallas_call x1, Pallas kernels, body(): pl.pallas_call(kernel, out_shape=jax.ShapeDtypeStruct((4, 16, 128), jnp.f...  18.3 us
    unnamed x1, local copies, waits for them, and re-layouts  0.62 us

profile of v1, /device:TPU:225, one launch (start us, length us, event | category | flops | bytes accessed | tf_op | source)
XLA Modules:
  0.0 18.9 jit_solution(3026210385011908663)
XLA Ops:
  0.0 18.3 %shard_map.73 = f32[4,16,128]{2,1,0:T(8,128)S(1)} custom-call(bf16[1,4,128,256]{3,2,1,0:T(8,128)(2,1)} %den.1, s32[1,4,128,256]{3,2,1,0:T(8,128)} %mat.1, f32[3,8]{1,0:T(4,128)} %bitcast.3, f32[8]{0:T(128)} %opa.1, f32[8]{0:T(128)} %cen.1, f32[1,4,4]{2,1,0:T(4,128)} %wts.1, s32[1,5]{1,0:T(1,128)} %flg.1), custom_call_target="tpu_custom_call" | custom-call | tf_op jit(solution)/shard_map/pallas_call | solution.py:710
  18.3 0.6 %copy.10 = f32[4,1,2048]{2,1,0:T(1,128)} copy(f32[4,1,2048]{2,1,0:T(1,128)S(1)} %bitcast.2) | data formatting | bytes 65536
